TPU v7x, 512 devices: a whole 4x8x8 slice. The times are simulated.
512 devices in a mesh: ctx: 16 (over x, z_hi), dp: 8 (over y), tp: 4 (over z_lo, core).
Axes of the slice: x: 4, y: 8, z: 8 (z_hi: 4, z_lo: 2; z = z_hi * 2 + z_lo), core: 2. Of those that a mesh axis runs over, the one named last changes fastest.
Arguments:
- token_ids: int32 [4, 16], replicated, may hold values from 0 to 50279
- decode_prompt: int32 [16], replicated, may hold values from 0 to 15, as said below
- embedding: bfloat16 [50280, 4096], P('dp', ('ctx', 'tp')), may hold values from -6 to 6
- norm_gain: float32 [4096], replicated, may hold values from 0.1 to 1.9
- w_zx: bfloat16 [2, 128, 64, 4096], P(None, ('tp', 'ctx')), may hold values from -0.09375 to 0.09375
- w_bcdt: bfloat16 [4096, 384], P(None, ('ctx', 'tp')), may hold values from -0.09375 to 0.09375
- conv_x_weight: float32 [4, 128, 64], P(None, ('tp', 'ctx')), may hold values from -3 to 3
- conv_x_bias: float32 [128, 64], P(('tp', 'ctx')), may hold values from -3 to 3
- conv_bc_weight: float32 [4, 256], replicated, may hold values from -3 to 3
- conv_bc_bias: float32 [256], replicated, may hold values from -3 to 3
- dt_bias: float32 [128], P(('tp', 'ctx')), may hold values from -4 to -1
- a_log: float32 [128], P(('tp', 'ctx')), may hold values from 0 to 2.7
- d_skip: float32 [128], P(('tp', 'ctx')), may hold values from 0.5 to 1.5
- gate_norm_gain: float32 [128, 64], P(('tp', 'ctx')), may hold values from 0.1 to 1.9
- w_out: bfloat16 [128, 64, 4096], P(('tp', 'ctx')), may hold values from -0.0625 to 0.0625
- state_parts: bfloat16 [16, 16, 128, 64, 128], P('ctx', 'dp', 'tp'), may hold values from -6 to 6
- seg_rate: float32 [16, 16, 128], P('ctx', 'dp', 'tp'), may hold values from 0 to 2
- x_tail: bfloat16 [16, 3, 128, 64], P('dp', None, ('tp', 'ctx')), may hold values from -6 to 6
- bc_tail: bfloat16 [16, 3, 256], P('dp'), may hold values from -6 to 6
Outputs:
- mixer_out: bfloat16 [4, 16, 4096], P(None, 'dp', ('ctx', 'tp'))
- final_state: float32 [16, 128, 64, 128], P('dp', ('tp', 'ctx'))
Inputs may be any that keep to these rules, and one draw needn't show every extreme that they name: decode_prompt is a permutation of the prompts; slot s is decoded by dp group s // 2, and prompt q is held by dp group q // 2; the 2 prompts held by one dp group are decoded by 2 different dp groups.
All inputs are finite; a program needn't handle non-finite values.
Results may differ from a plain program's by a relative error of at most 0.02.
Values may be sent and summed in bfloat16 or wider, within the bound.
No kernel may reach another device: no remote copies, remote signals or barrier semaphores. Data moves between devices by JAX's collectives and lax.ppermute only.
A program may use at most 64 MiB of HBM per device.

v0:
```python
import jax
import jax.numpy as jnp
from jax import lax
from jax.sharding import PartitionSpec as P

HEADS = 128
HEAD_DIM = 64
EPS = 1e-05
BOTH = ("ctx", "tp")
BF = jnp.bfloat16
F32 = jnp.float32


def exchange(pieces, axis):
    return lax.all_to_all(pieces, axis, 0, 0, tiled=True)


def in_three(values):
    first = values.astype(BF)
    rest = values - first.astype(F32)
    second = rest.astype(BF)
    third = (rest - second.astype(F32)).astype(BF)
    return (first, second, third)


def per_device(
    token_ids,
    decode_prompt,
    embedding,
    norm_gain,
    w_zx,
    w_bcdt,
    conv_x_weight,
    conv_x_bias,
    conv_bc_weight,
    conv_bc_bias,
    dt_bias,
    a_log,
    d_skip,
    gate_norm_gain,
    w_out,
    state_parts,
    seg_rate,
    x_tail,
    bc_tail,
):
    ctx, group, tp = (lax.axis_index(a) for a in ("ctx", "dp", "tp"))
    n_ctx, n_dp, n_tp = (lax.axis_size(a) for a in ("ctx", "dp", "tp"))
    slots = state_parts.shape[1]
    heads = w_zx.shape[1]
    state_width = state_parts.shape[-1]
    steps = token_ids.shape[0]
    vocab_rows, features = embedding.shape
    model = norm_gain.shape[0]
    rows = steps * slots
    channels = heads * HEAD_DIM
    block = features * n_tp
    states = state_parts[0].reshape(slots, n_ctx, heads, HEAD_DIM, state_width)
    states = jnp.swapaxes(states, 0, 1).reshape(n_ctx, -1, state_width)
    own_columns = w_bcdt.shape[1]
    w_pieces = w_bcdt.T.reshape(own_columns, n_ctx, block)
    w_pieces = jnp.swapaxes(w_pieces, 0, 1).reshape(n_ctx, -1, state_width)
    rates = jnp.swapaxes(seg_rate[0].reshape(slots, n_ctx, heads), 0, 1)
    rates = jnp.stack(in_three(rates), axis=1).reshape(n_ctx, -1, 1)
    rates = jnp.broadcast_to(rates, (*rates.shape[:2], state_width))
    state_rows, w_rows, rate_rows = (states.shape[1], w_pieces.shape[1], rates.shape[1])
    sent = jnp.concatenate([states, w_pieces, rates], axis=1)
    filler = -sent.shape[1] % 16
    sent = jnp.pad(sent, ((0, 0), (0, filler), (0, 0)))
    got = exchange(sent, "ctx")
    prompts = decode_prompt.shape[0]
    chosen = (decode_prompt[:, None] == jnp.arange(prompts)[None, :]).astype(jnp.int32)
    tokens = jnp.sum(token_ids[:, None, :] * chosen[None], axis=2)
    tokens = jnp.swapaxes(tokens.reshape(steps, n_dp, slots), 0, 1).reshape(-1)
    hot = (tokens[:, None] - group * vocab_rows == jnp.arange(vocab_rows)[None, :]).astype(BF)
    found = jnp.dot(hot, embedding, preferred_element_type=F32).astype(BF)
    found = lax.psum(found, "dp")
    own = lax.dynamic_slice_in_dim(found, group * rows, rows)
    beside = lax.all_gather(own, "tp")
    near = jnp.swapaxes(beside, 0, 1).reshape(rows, block).astype(F32)
    near_gain = lax.dynamic_slice_in_dim(norm_gain, ctx * block, block)
    w_block = got[:, state_rows : state_rows + w_rows].reshape(-1, block)
    partial = lax.dot_general(
        (near * near_gain).astype(BF), w_block, (((1,), (1,)), ((), ())), preferred_element_type=F32
    ).astype(BF)
    piece = jnp.concatenate([own.reshape(-1, 128), partial.reshape(-1, 128)], axis=0)
    own_rows = own.size // 128
    everyone = exchange(jnp.broadcast_to(piece[None], (n_ctx * n_tp, *piece.shape)), BOTH)
    parts = got[:, state_rows + w_rows : state_rows + w_rows + rate_rows, 0].astype(F32)
    parts = parts.reshape(n_ctx, 3, slots, heads)
    rate = parts[:, 0] + parts[:, 1] + parts[:, 2]
    later = jnp.cumsum(rate[::-1], axis=0)[::-1] - rate
    weight = jnp.exp(-later)[..., None, None]
    scaled = weight * got[:, :state_rows].reshape(
        n_ctx, slots, heads, HEAD_DIM, state_width
    ).astype(F32)
    combined = jnp.sum(scaled.astype(BF).astype(F32), axis=0).astype(BF)
    bundle = jnp.concatenate(
        [
            combined.reshape(slots, -1, 128),
            jnp.swapaxes(x_tail, 1, 1).reshape(slots, -1, 128),
            bc_tail.reshape(slots, -1, 128),
        ],
        axis=1,
    )
    bundle = jnp.pad(bundle, ((0, 0), (0, -bundle.shape[1] % 16), (0, 0)))
    wanted = decode_prompt.reshape(n_dp, slots) - group * slots
    second = jnp.any(wanted == 1, axis=1)
    routed = jnp.where(second[:, None, None], bundle[1][None], bundle[0][None])
    arrived = exchange(routed, "dp")
    taken = everyone[:, :own_rows].reshape(n_ctx * n_tp, rows, features)
    flat = jnp.swapaxes(taken, 0, 1).reshape(rows, model).astype(F32)
    inverse = lax.rsqrt(jnp.mean(flat * flat, axis=-1, keepdims=True) + EPS)
    normed = (flat * inverse * norm_gain).astype(BF)
    projected = jnp.einsum("rd,khed->krhe", normed, w_zx, preferred_element_type=F32)
    projected = projected.reshape(2, steps, slots, heads, HEAD_DIM)
    sums = everyone[:, own_rows:].reshape(n_ctx, n_tp, rows, n_ctx, own_columns).astype(F32)
    sums = jnp.sum(sums, axis=0).transpose(1, 2, 0, 3).reshape(rows, -1)
    columns = (sums * inverse).reshape(steps, slots, -1)
    own_slots = lax.dynamic_slice_in_dim(decode_prompt, group * slots, slots)
    taken = jnp.stack(
        [
            lax.dynamic_index_in_dim(arrived, own_slots[s] // slots, 0, keepdims=False)
            for s in range(slots)
        ]
    ).astype(F32)
    at = combined.size // slots // 128
    ssm_state = taken[:, :at].reshape(slots, heads, HEAD_DIM, state_width)
    tail_rows = x_tail.size // slots // 128
    x_window = taken[:, at : at + tail_rows].reshape(slots, 3, heads, HEAD_DIM)
    bc_rows = bc_tail.size // slots // 128
    bc_window = taken[:, at + tail_rows : at + tail_rows + bc_rows].reshape(slots, 3, -1)
    head_start = 2 * state_width + (tp * n_ctx + ctx) * heads
    dt_raw = lax.dynamic_slice_in_dim(columns, head_start, heads, 2)
    decay_rate = -jnp.exp(a_log)
    gated_steps = []
    for moment in range(steps):
        x_window = jnp.concatenate([x_window, projected[1, moment][:, None]], axis=1)
        bc_window = jnp.concatenate(
            [bc_window, columns[moment, :, None, : 2 * state_width]], axis=1
        )
        x_conv = jax.nn.silu(jnp.einsum("pkhe,khe->phe", x_window, conv_x_weight) + conv_x_bias)
        bc_conv = jax.nn.silu(jnp.einsum("pkn,kn->pn", bc_window, conv_bc_weight) + conv_bc_bias)
        step_size = jax.nn.softplus(dt_raw[moment] + dt_bias)
        retain = jnp.exp(step_size * decay_rate)
        ssm_state = (
            retain[:, :, None, None] * ssm_state
            + (step_size[:, :, None] * x_conv)[:, :, :, None] * bc_conv[:, None, None, :state_width]
        )
        output = (
            jnp.einsum("phen,pn->phe", ssm_state, bc_conv[:, state_width:])
            + d_skip[None, :, None] * x_conv
        )
        gated_steps.append(output * jax.nn.silu(projected[0, moment]))
        x_window = x_window[:, 1:]
        bc_window = bc_window[:, 1:]
    gated = jnp.stack(gated_steps).reshape(rows, channels)
    squares = jnp.sum(gated * gated, axis=1)
    weighted = (gated * gate_norm_gain.reshape(-1)).astype(BF)
    partial_out = jnp.dot(weighted, w_out.reshape(channels, model), preferred_element_type=F32)
    partial_out = jnp.swapaxes(partial_out.reshape(rows, n_ctx * n_tp, -1), 0, 1)
    partial_out = partial_out.reshape(n_ctx * n_tp, -1, 128).astype(BF)
    square_parts = jnp.concatenate(in_three(squares))
    square_parts = jnp.pad(square_parts, (0, 128 * 4 - square_parts.shape[0])).reshape(1, 4, 128)
    outgoing = jnp.concatenate(
        [partial_out, jnp.broadcast_to(square_parts, (n_ctx * n_tp, 4, 128))], axis=1
    )
    incoming = jnp.sum(exchange(outgoing, BOTH).astype(F32), axis=0)
    out_rows = partial_out.shape[1]
    total = jnp.sum(incoming[out_rows, : 3 * rows].reshape(3, rows), axis=0)
    scale = lax.rsqrt(total / (HEADS * HEAD_DIM) + EPS)
    mixed = incoming[:out_rows].reshape(rows, -1) * scale[:, None]
    return (mixed.reshape(steps, slots, -1).astype(BF), ssm_state)


def solution(mesh):
    return jax.shard_map(
        per_device,
        mesh=mesh,
        in_specs=(
            P(),
            P(),
            P("dp", ("ctx", "tp")),
            P(),
            P(None, ("tp", "ctx"), None, None),
            P(None, ("ctx", "tp")),
            P(None, ("tp", "ctx"), None),
            P(("tp", "ctx"), None),
            P(),
            P(),
            P(("tp", "ctx")),
            P(("tp", "ctx")),
            P(("tp", "ctx")),
            P(("tp", "ctx"), None),
            P(("tp", "ctx"), None, None),
            P("ctx", "dp", "tp", None, None),
            P("ctx", "dp", "tp"),
            P("dp", None, ("tp", "ctx"), None),
            P("dp", None, None),
        ),
        out_specs=(P(None, "dp", ("ctx", "tp")), P("dp", ("tp", "ctx"), None, None)),
        check_vma=False,
    )
```

profile of v0, /device:TPU:1, one launch (start us, length us, event | category | flops | bytes accessed | tf_op | source)
XLA Modules:
  0.0 135.3 jit_solution(1942876022011710154)
XLA Ops:
  0.7 0.9 reshape_squeeze.10
  1.8 1.3 copy.239
  3.3 1.1 fusion.5
  4.5 13.4 %all-to-all-start = ((bf16[16,288,128]{2,1,0:T(8,128)(2,1)}), bf16[16,288,128]{2,1,0:T(8,128)(2,1)S(1)}, u32[]{:S(2)}, u32[]{:S(2)}) async-start(bf16[16,288,128]{2,1,0:T(8,128)(2,1)} %fusion.5), calls=%async_computation | async-start | bytes 2359296 | tf_op jit(solution)/shard_map/all_to_all | solution.py:15
  23.8 0.6 reshape.447
  24.4 0.7 reshape.486
  25.8 0.8 dynamic_slice.20
  26.6 1.6 %fusion.7 = bf16[64,64]{1,0:T(8,128)(2,1)S(1)} fusion(bf16[6285,64]{0,1:T(8,128)(2,1)} %param.21, s32[64]{0:T(128)S(1)} %sub.53), kind=kOutput, calls=%fused_computation.11 | convolution fusion | flops 51893056 | bytes 812928 | tf_op jit(solution)/shard_map/dot_general | solution.py:76
  28.2 24.6 %psum.7 = bf16[64,64]{1,0:T(8,128)(2,1)S(1)} all-reduce(bf16[64,64]{1,0:T(8,128)(2,1)S(1)} %fusion.7), channel_id=1, replica_groups=mesh['ctx'=16,'dp'=8,'tp'=4] {'dp'}, use_global_device_ids=true, to_apply=%region_1.2 | all-reduce | flops 4096 | bytes 16384 | tf_op jit(solution)/shard_map/psum | solution.py:77
  52.9 11.7 %all-gather = bf16[32,64]{1,0:T(8,128)(2,1)S(1)} all-gather(bf16[8,64]{1,0:T(8,128)(2,1)S(1)} %constant_dynamic-slice_fusion.6), channel_id=2, replica_groups=mesh['ctx'=16,'dp'=8,'tp'=4] {'tp'}, dimensions={0}, use_global_device_ids=true | all-gather | bytes 5120 | tf_op jit(solution)/shard_map/all_gather | solution.py:79
  64.7 2.3 %copy.273 = bf16[4096,128]{1,0:T(8,128)(2,1)} copy(bf16[4096,128]{0,1:T(8,128)(2,1)} %bitcast.343) | data formatting | bytes 2097152 | tf_op jit(solution)/shard_map/dot_general | solution.py:160
  66.9 0.6 reduce_or.9
  69.4 0.7 broadcast_in_dim.40
  70.1 10.3 %all-to-all-start.1 = ((bf16[64,10,128]{2,1,0:T(8,128)(2,1)}), bf16[64,10,128]{2,1,0:T(8,128)(2,1)S(1)}, u32[]{:S(2)}, u32[]{:S(2)}) async-start(bf16[64,10,128]{2,1,0:T(8,128)(2,1)} %broadcast_in_dim.40), calls=%async_computation.1 | async-start | bytes 524288 | tf_op jit(solution)/shard_map/all_to_all | solution.py:15
  80.4 0.7 fusion.8
  81.1 0.7 fusion.16
  81.8 1.4 %broadcast_select_fusion = bf16[8,144,128]{2,1,0:T(8,128)(2,1)} fusion(pred[8]{0:T(512)(128)(4,1)} %reduce_or.9, bf16[144,128]{1,0:T(8,128)(2,1)S(1)} %get-tuple-element.31, bf16[144,128]{1,0:T(8,128)(2,1)S(1)} %get-tuple-element.30), kind=kLoop, calls=%fused_computation.15 | loop fusion | flops 147456 | bytes 368648 | tf_op jit(solution)/shard_map/jit(_where)/select_n | solution.py:109
  83.2 9.1 %all-to-all-done.1 = bf16[64,10,128]{2,1,0:T(8,128)(2,1)S(1)} async-done(((bf16[64,10,128]{2,1,0:T(8,128)(2,1)}), bf16[64,10,128]{2,1,0:T(8,128)(2,1)S(1)}, u32[]{:S(2)}, u32[]{:S(2)}) %all-to-all-start.1) | async-done | bytes 163872 | tf_op jit(solution)/shard_map/all_to_all | solution.py:15
  92.4 4.1 %all-to-all-start.2 = ((bf16[8,144,128]{2,1,0:T(8,128)(2,1)}), bf16[8,144,128]{2,1,0:T(8,128)(2,1)}, u32[]{:S(2)}, u32[]{:S(2)}) async-start(bf16[8,144,128]{2,1,0:T(8,128)(2,1)} %broadcast_select_fusion), calls=%async_computation.2 | async-start | bytes 589824 | tf_op jit(solution)/shard_map/all_to_all | solution.py:15
  97.4 5.7 %reshape.454 = f32[16,4,8,16,6]{4,3,2,1,0:T(8,128)} reshape(f32[64,6,128]{2,1,0:T(8,128)S(1)} %slice_convert_fusion) | data formatting | bytes 393216 | tf_op jit(solution)/shard_map/convert_element_type | solution.py:117
  103.1 2.6 %reduce_sum.76 = f32[4,8,16,6]{3,2,1,0:T(8,128)S(1)} reduce(f32[16,4,8,16,6]{4,3,2,1,0:T(8,128)} %reshape.454, f32[]{:T(128)} %constant.87.clone.1), dimensions={0}, to_apply=%region_2.3 | reduce | flops 46080 | bytes 208900 | tf_op jit(solution)/shard_map/reduce_sum | solution.py:118
  106.3 0.6 slice_bitcast_fusion.3
  107.3 1.7 %fusion.18 = f32[8,2,2,64]{3,0,2,1:T(8,128)S(1)} fusion(bf16[2,2,64,4096]{3,2,1,0:T(8,128)(2,1)S(1)} %copy-done, f32[8,4096]{1,0:T(8,128)S(1)} %reshape.456, f32[4096]{0:T(1024)} %param.22, f32[8]{0:T(128)} %copy-done.16), kind=kOutput, calls=%fused_computation.35 | convolution fusion | flops 16875520 | bytes 2252832 | tf_op jit(solution)/shard_map/rd,khed->krhe/dot_general | solution.py:115
  109.1 1.4 %multiply_exponential_fusion.3 = (f32[2,2]{1,0:T(2,128)S(1)}, f32[2,2]{1,0:T(2,128)S(1)}, f32[2,2]{1,0:T(2,128)S(1)}, f32[2,2]{1,0:T(2,128)S(1)}, f32[2,2]{1,0:T...) fusion(f32[2]{0:T(128)} %exponential_negate_fusion, f32[2]{0:T(128)} %param.29, ...), kind=kLoop, calls=%fused_computation.217 | loop fusion | flops 128 | bytes 224 | tf_op jit(solution)/shard_map/exp | solution.py:145
  111.0 0.8 constant_dynamic-slice_fusion.4
  112.0 0.8 broadcast_multiply_fusion.4
  113.8 0.9 multiply_add_fusion
  114.9 0.7 fusion.87
  115.7 0.7 multiply_convert_fusion.2
  116.4 0.9 fusion.6
  117.9 16.4 %all_to_all.20 = bf16[64,8,128]{2,1,0:T(8,128)(2,1)S(1)} all-to-all(bf16[64,8,128]{2,1,0:T(8,128)(2,1)S(1)} %pad_maximum_fusion), channel_id=1, replica_groups=mesh['ctx'=16,'dp'=8,'tp'=4] {'ctx','tp'}, dimensions={0} | all-to-all | bytes 262144 | tf_op jit(solution)/shard_map/all_to_all | solution.py:15
  134.7 0.7 multiply_convert_fusion.3
  (155 shorter events, 8.2 us)
Async XLA Ops:
  0.6 106.7 %copy-start = (bf16[2,2,64,4096]{3,2,1,0:T(8,128)(2,1)S(1)}, bf16[2,2,64,4096]{3,2,1,0:T(8,128)(2,1)}, u32[]{:S(2)}) copy-start(bf16[2,2,64,4096]{3,2,1,0:T(8,128)(2,1)} %param.23) | copy-start | bytes 6291460
  0.6 2.5 %copy-start.3 = (bf16[4096,6]{0,1:T(8,128)(2,1)S(1)}, bf16[4096,6]{0,1:T(8,128)(2,1)}, u32[]{:S(2)}) copy-start(bf16[4096,6]{0,1:T(8,128)(2,1)} %param.24) | copy-start | bytes 147460
  3.3 14.6 %copy-start.19 = (s32[16]{0:T(128)S(1)}, s32[16]{0:T(128)}, u32[]{:S(2)}) copy-start(s32[16]{0:T(128)} %param.20) | copy-start | bytes 196
  3.3 20.5 %copy-start.14 = (bf16[2,3,256]{2,0,1:T(2,128)(2,1)S(1)}, bf16[2,3,256]{2,0,1:T(2,128)(2,1)}, u32[]{:S(2)}) copy-start(bf16[2,3,256]{2,0,1:T(2,128)(2,1)} %param.37) | copy-start | bytes 9220
  3.3 21.1 %copy-start.15 = (bf16[2,3,2,64]{3,2,1,0:T(2,128)(2,1)S(1)}, bf16[2,3,2,64]{3,2,1,0:T(2,128)(2,1)}, u32[]{:S(2)}) copy-start(bf16[2,3,2,64]{3,2,1,0:T(2,128)(2,1)} %param.36) | copy-start | bytes 4612
  3.3 21.9 %copy-start.17 = (s32[4,16]{1,0:T(4,128)S(1)}, s32[4,16]{1,0:T(4,128)}, u32[]{:S(2)}) copy-start(s32[4,16]{1,0:T(4,128)} %param.19) | copy-start | bytes 772
  4.5 63.7 %all-to-all-start = ((bf16[16,288,128]{2,1,0:T(8,128)(2,1)}), bf16[16,288,128]{2,1,0:T(8,128)(2,1)S(1)}, u32[]{:S(2)}, u32[]{:S(2)}) async-start(bf16[16,288,128]{2,1,0:T(8,128)(2,1)} %fusion.5), calls=%async_computation | async-start | bytes 2359296 | tf_op jit(solution)/shard_map/all_to_all | solution.py:15
  17.9 49.7 %copy-start.20 = (f32[2]{0:T(128)S(1)}, f32[2]{0:T(128)}, u32[]{:S(2)}) copy-start(f32[2]{0:T(128)} %param.30) | copy-start | bytes 28
  70.1 22.3 %all-to-all-start.1 = ((bf16[64,10,128]{2,1,0:T(8,128)(2,1)}), bf16[64,10,128]{2,1,0:T(8,128)(2,1)S(1)}, u32[]{:S(2)}, u32[]{:S(2)}) async-start(bf16[64,10,128]{2,1,0:T(8,128)(2,1)} %broadcast_in_dim.40), calls=%async_computation.1 | async-start | bytes 524288 | tf_op jit(solution)/shard_map/all_to_all | solution.py:15
  92.4 18.6 %all-to-all-start.2 = ((bf16[8,144,128]{2,1,0:T(8,128)(2,1)}), bf16[8,144,128]{2,1,0:T(8,128)(2,1)}, u32[]{:S(2)}, u32[]{:S(2)}) async-start(bf16[8,144,128]{2,1,0:T(8,128)(2,1)} %broadcast_select_fusion), calls=%async_computation.2 | async-start | bytes 589824 | tf_op jit(solution)/shard_map/all_to_all | solution.py:15
  96.7 0.5 copy-start.16
  106.3 0.6 copy-start.4
  106.9 3.6 %copy-start.8 = (f32[2,1,256]{2,0,1:T(2,128)S(1)}, f32[2,1,256]{2,0,1:T(2,128)}, u32[]{:S(2)}) copy-start(f32[2,1,256]{2,0,1:T(2,128)} %get-tuple-element.49) | copy-start | bytes 6148
  106.9 3.6 %copy-start.7 = (f32[2,1,256]{2,0,1:T(2,128)S(1)}, f32[2,1,256]{2,0,1:T(2,128)}, u32[]{:S(2)}) copy-start(f32[2,1,256]{2,0,1:T(2,128)} %get-tuple-element.48) | copy-start | bytes 6148
  106.9 3.6 %copy-start.6 = (f32[2,1,256]{2,0,1:T(2,128)S(1)}, f32[2,1,256]{2,0,1:T(2,128)}, u32[]{:S(2)}) copy-start(f32[2,1,256]{2,0,1:T(2,128)} %get-tuple-element.47) | copy-start | bytes 6148
  106.9 3.6 %copy-start.5 = (f32[2,1,256]{2,0,1:T(2,128)S(1)}, f32[2,1,256]{2,0,1:T(2,128)}, u32[]{:S(2)}) copy-start(f32[2,1,256]{2,0,1:T(2,128)} %get-tuple-element.46) | copy-start | bytes 6148
  107.1 4.9 %copy-start.12 = (f32[4,2,64]{2,1,0:T(2,128)S(1)}, f32[4,2,64]{2,1,0:T(2,128)}, u32[]{:S(2)}) copy-start(f32[4,2,64]{2,1,0:T(2,128)} %param.25) | copy-start | bytes 6148
  107.1 5.8 %copy-start.13 = (f32[4,256]{1,0:T(4,128)S(1)}, f32[4,256]{1,0:T(4,128)}, u32[]{:S(2)}) copy-start(f32[4,256]{1,0:T(4,128)} %param.27) | copy-start | bytes 12292
  107.1 5.8 %copy-start.18 = (f32[256]{0:T(256)S(1)}, f32[256]{0:T(256)}, u32[]{:S(2)}) copy-start(f32[256]{0:T(256)} %param.28) | copy-start | bytes 3076
  107.3 9.1 %copy-start.1 = (bf16[4096,128]{1,0:T(8,128)(2,1)S(1)}, bf16[4096,128]{1,0:T(8,128)(2,1)}, u32[]{:S(2)}) copy-start(bf16[4096,128]{1,0:T(8,128)(2,1)} %copy.273) | copy-start | bytes 3145732
  110.5 3.3 %copy-start.9 = (f32[2,2]{1,0:T(2,128)}, f32[2,2]{1,0:T(2,128)S(1)}, u32[]{:S(2)}) copy-start(f32[2,2]{1,0:T(2,128)S(1)} %get-tuple-element.14) | copy-start | bytes 52
  110.5 3.3 %copy-start.10 = (f32[2,2]{1,0:T(2,128)}, f32[2,2]{1,0:T(2,128)S(1)}, u32[]{:S(2)}) copy-start(f32[2,2]{1,0:T(2,128)S(1)} %get-tuple-element.40) | copy-start | bytes 52
  110.5 3.3 %copy-start.11 = (f32[2,2]{1,0:T(2,128)}, f32[2,2]{1,0:T(2,128)S(1)}, u32[]{:S(2)}) copy-start(f32[2,2]{1,0:T(2,128)S(1)} %get-tuple-element.42) | copy-start | bytes 52
  114.7 20.6 %copy-start.2 = (f32[2,2,64,128]{3,2,1,0:T(8,128)}, f32[2,2,64,128]{3,2,1,0:T(8,128)S(1)}, u32[]{:S(2)}) copy-start(f32[2,2,64,128]{3,2,1,0:T(8,128)S(1)} %multiply_add_fusion) | copy-start | bytes 393220
where the time goes:
time: 136 us; the launch traced here: 135 us
  blocking collectives  52.7 us (39%)
  starting transfers between devices  27.8 us (20%)
  local copies, waits for them, and re-layouts  19.7 us (14%)
  other arithmetic  14.2 us (10%)
  waiting for transfers between devices  9.13 us (7%)
  between operations  6.49 us (5%)
  matrix products  5.28 us (4%)
    all_to_all x3, starting transfers between devices, exchange(): return lax.all_to_all(pieces, axis, 0, 0, tiled=True)  27.8 us
    psum x1, blocking collectives, per_device(): found = lax.psum(found, 'dp')  24.6 us
    all_to_all x1, blocking collectives, exchange(): return lax.all_to_all(pieces, axis, 0, 0, tiled=True)  16.4 us
    all_gather x1, blocking collectives, per_device(): beside = lax.all_gather(own, 'tp')  11.7 us
    all_to_all x3, waiting for transfers between devices, exchange(): return lax.all_to_all(pieces, axis, 0, 0, tiled=True)  9.13 us
    convert_element_type x1, local copies, waits for them, and re-layouts, per_device(): everyone[:, own_rows:].reshape(n_ctx, n_tp, rows, n_ctx, own_columns)  5.71 us
  transfers between devices with their start and end apart: 3, of which 1 were waited for; matrix products, arithmetic and copies ran while one was open for 19% of the time, Pallas kernels for 0%

commit v1 on v0

--- a/solution.py
+++ b/solution.py
@@ -74,7 +74,7 @@
     tokens = jnp.swapaxes(tokens.reshape(steps, n_dp, slots), 0, 1).reshape(-1)
     hot = (tokens[:, None] - group * vocab_rows == jnp.arange(vocab_rows)[None, :]).astype(BF)
     found = jnp.dot(hot, embedding, preferred_element_type=F32).astype(BF)
-    found = lax.psum(found, "dp")
+    found = jnp.sum(lax.all_gather(found, "dp"), axis=0)
     own = lax.dynamic_slice_in_dim(found, group * rows, rows)
     beside = lax.all_gather(own, "tp")
     near = jnp.swapaxes(beside, 0, 1).reshape(rows, block).astype(F32)

time: 136 us -> 133 us (0.978)
  blocking collectives: 52.7 us -> 48.5 us
    psum x1 -> x0, blocking collectives: 24.6 us -> none  [per_device(): found = lax.psum(found, 'dp')]
    all_gather x0 -> x1, blocking collectives: none -> 21.1 us  [per_device(): found = jnp.sum(lax.all_gather(found, 'dp'), axis=0)]
where the time goes in v1:
time: 133 us; the launch traced here: 132 us
  blocking collectives  48.5 us (36%)
  starting transfers between devices  29 us (22%)
  local copies, waits for them, and re-layouts  19.7 us (15%)
  other arithmetic  14.3 us (11%)
  waiting for transfers between devices  9.13 us (7%)
  between operations  6.49 us (5%)
  matrix products  5.28 us (4%)
    all_to_all x3, starting transfers between devices, exchange(): return lax.all_to_all(pieces, axis, 0, 0, tiled=True)  29 us
    all_gather x1, blocking collectives, per_device(): found = jnp.sum(lax.all_gather(found, 'dp'), axis=0)  21.1 us
    all_to_all x1, blocking collectives, exchange(): return lax.all_to_all(pieces, axis, 0, 0, tiled=True)  16.5 us
    all_gather x1, blocking collectives, per_device(): beside = lax.all_gather(own, 'tp')  10.9 us
    all_to_all x3, waiting for transfers between devices, exchange(): return lax.all_to_all(pieces, axis, 0, 0, tiled=True)  9.13 us
    convert_element_type x1, local copies, waits for them, and re-layouts, per_device(): everyone[:, own_rows:].reshape(n_ctx, n_tp, rows, n_ctx, own_columns)  5.71 us
  transfers between devices with their start and end apart: 3, of which 1 were waited for; matrix products, arithmetic and copies ran while one was open for 19% of the time, Pallas kernels for 0%

profile of v1, /device:TPU:1, one launch (start us, length us, event | category | flops | bytes accessed | tf_op | source)
XLA Modules:
  0.0 132.4 jit_solution(2021530369447569469)
XLA Ops:
  0.7 0.9 reshape_squeeze.10
  1.8 1.3 copy.238
  3.3 1.1 fusion.5
  4.5 13.4 %all-to-all-start = ((bf16[16,288,128]{2,1,0:T(8,128)(2,1)}), bf16[16,288,128]{2,1,0:T(8,128)(2,1)S(1)}, u32[]{:S(2)}, u32[]{:S(2)}) async-start(bf16[16,288,128]{2,1,0:T(8,128)(2,1)} %fusion.5), calls=%async_computation | async-start | bytes 2359296 | tf_op jit(solution)/shard_map/all_to_all | solution.py:15
  23.8 0.6 reshape.447
  24.4 0.7 reshape.487
  25.8 0.8 dynamic_slice.20
  26.6 1.6 %fusion.7 = bf16[64,64]{1,0:T(8,128)(2,1)S(1)} fusion(bf16[6285,64]{0,1:T(8,128)(2,1)} %param.21, s32[64]{0:T(128)S(1)} %sub.53), kind=kOutput, calls=%fused_computation.11 | convolution fusion | flops 51893056 | bytes 812928 | tf_op jit(solution)/shard_map/dot_general | solution.py:76
  28.2 21.1 %all-gather = bf16[512,64]{1,0:T(8,128)(2,1)S(1)} all-gather(bf16[64,64]{1,0:T(8,128)(2,1)S(1)} %fusion.7), channel_id=2, replica_groups=mesh['ctx'=16,'dp'=8,'tp'=4] {'dp'}, dimensions={0}, use_global_device_ids=true | all-gather | bytes 73728 | tf_op jit(solution)/shard_map/all_gather | solution.py:77
  49.4 10.9 %all-gather.1 = bf16[32,64]{1,0:T(8,128)(2,1)S(1)} all-gather(bf16[8,64]{1,0:T(8,128)(2,1)S(1)} %constant_dynamic-slice_fusion.6), channel_id=3, replica_groups=mesh['ctx'=16,'dp'=8,'tp'=4] {'tp'}, dimensions={0}, use_global_device_ids=true | all-gather | bytes 5120 | tf_op jit(solution)/shard_map/all_gather | solution.py:79
  60.5 2.3 %copy.272 = bf16[4096,128]{1,0:T(8,128)(2,1)} copy(bf16[4096,128]{0,1:T(8,128)(2,1)} %bitcast.344) | data formatting | bytes 2097152 | tf_op jit(solution)/shard_map/dot_general | solution.py:160
  62.8 0.6 reduce_or.9
  65.2 0.7 broadcast_in_dim.40
  65.9 10.3 %all-to-all-start.1 = ((bf16[64,10,128]{2,1,0:T(8,128)(2,1)}), bf16[64,10,128]{2,1,0:T(8,128)(2,1)S(1)}, u32[]{:S(2)}, u32[]{:S(2)}) async-start(bf16[64,10,128]{2,1,0:T(8,128)(2,1)} %broadcast_in_dim.40), calls=%async_computation.1 | async-start | bytes 524288 | tf_op jit(solution)/shard_map/all_to_all | solution.py:15
  76.3 0.7 fusion.8
  77.0 0.7 fusion.16
  77.7 1.4 %broadcast_select_fusion = bf16[8,144,128]{2,1,0:T(8,128)(2,1)} fusion(pred[8]{0:T(512)(128)(4,1)} %reduce_or.9, bf16[144,128]{1,0:T(8,128)(2,1)S(1)} %get-tuple-element.31, bf16[144,128]{1,0:T(8,128)(2,1)S(1)} %get-tuple-element.30), kind=kLoop, calls=%fused_computation.15 | loop fusion | flops 147456 | bytes 368648 | tf_op jit(solution)/shard_map/jit(_where)/select_n | solution.py:109
  79.1 9.1 %all-to-all-done.1 = bf16[64,10,128]{2,1,0:T(8,128)(2,1)S(1)} async-done(((bf16[64,10,128]{2,1,0:T(8,128)(2,1)}), bf16[64,10,128]{2,1,0:T(8,128)(2,1)S(1)}, u32[]{:S(2)}, u32[]{:S(2)}) %all-to-all-start.1) | async-done | bytes 163872 | tf_op jit(solution)/shard_map/all_to_all | solution.py:15
  88.3 5.2 %all-to-all-start.2 = ((bf16[8,144,128]{2,1,0:T(8,128)(2,1)}), bf16[8,144,128]{2,1,0:T(8,128)(2,1)}, u32[]{:S(2)}, u32[]{:S(2)}) async-start(bf16[8,144,128]{2,1,0:T(8,128)(2,1)} %broadcast_select_fusion), calls=%async_computation.2 | async-start | bytes 589824 | tf_op jit(solution)/shard_map/all_to_all | solution.py:15
  94.5 5.7 %reshape.454 = f32[16,4,8,16,6]{4,3,2,1,0:T(8,128)} reshape(f32[64,6,128]{2,1,0:T(8,128)S(1)} %slice_convert_fusion) | data formatting | bytes 393216 | tf_op jit(solution)/shard_map/convert_element_type | solution.py:117
  100.2 2.6 %reduce_sum.89 = f32[4,8,16,6]{3,2,1,0:T(8,128)S(1)} reduce(f32[16,4,8,16,6]{4,3,2,1,0:T(8,128)} %reshape.454, f32[]{:T(128)} %constant.88.clone.1), dimensions={0}, to_apply=%region_2.3 | reduce | flops 46080 | bytes 208900 | tf_op jit(solution)/shard_map/reduce_sum | solution.py:118
  103.3 0.6 slice_bitcast_fusion.3
  104.4 1.7 %fusion.18 = f32[8,2,2,64]{3,0,2,1:T(8,128)S(1)} fusion(bf16[2,2,64,4096]{3,2,1,0:T(8,128)(2,1)S(1)} %copy-done, f32[8,4096]{1,0:T(8,128)S(1)} %reshape.456, f32[4096]{0:T(1024)} %param.22, f32[8]{0:T(128)} %copy-done.16), kind=kOutput, calls=%fused_computation.35 | convolution fusion | flops 16875520 | bytes 2252832 | tf_op jit(solution)/shard_map/rd,khed->krhe/dot_general | solution.py:115
  106.1 1.4 %multiply_exponential_fusion.3 = (f32[2,2]{1,0:T(2,128)S(1)}, f32[2,2]{1,0:T(2,128)S(1)}, f32[2,2]{1,0:T(2,128)S(1)}, f32[2,2]{1,0:T(2,128)S(1)}, f32[2,2]{1,0:T...) fusion(f32[2]{0:T(128)} %exponential_negate_fusion, f32[2]{0:T(128)} %param.29, ...), kind=kLoop, calls=%fused_computation.216 | loop fusion | flops 128 | bytes 224 | tf_op jit(solution)/shard_map/exp | solution.py:145
  108.0 0.8 constant_dynamic-slice_fusion.4
  109.1 0.8 broadcast_multiply_fusion.4
  110.9 0.9 multiply_add_fusion
  112.0 0.7 fusion.87
  112.7 0.7 multiply_convert_fusion.2
  113.5 0.9 fusion.6
  114.9 16.5 %all_to_all.20 = bf16[64,8,128]{2,1,0:T(8,128)(2,1)S(1)} all-to-all(bf16[64,8,128]{2,1,0:T(8,128)(2,1)S(1)} %pad_maximum_fusion), channel_id=1, replica_groups=mesh['ctx'=16,'dp'=8,'tp'=4] {'ctx','tp'}, dimensions={0} | all-to-all | bytes 262144 | tf_op jit(solution)/shard_map/all_to_all | solution.py:15
  131.8 0.7 multiply_convert_fusion.3
  (156 shorter events, 8.3 us)
Async XLA Ops:
  0.6 103.7 %copy-start = (bf16[2,2,64,4096]{3,2,1,0:T(8,128)(2,1)S(1)}, bf16[2,2,64,4096]{3,2,1,0:T(8,128)(2,1)}, u32[]{:S(2)}) copy-start(bf16[2,2,64,4096]{3,2,1,0:T(8,128)(2,1)} %param.23) | copy-start | bytes 6291460
  0.6 2.5 %copy-start.3 = (bf16[4096,6]{0,1:T(8,128)(2,1)S(1)}, bf16[4096,6]{0,1:T(8,128)(2,1)}, u32[]{:S(2)}) copy-start(bf16[4096,6]{0,1:T(8,128)(2,1)} %param.24) | copy-start | bytes 147460
  3.3 14.6 %copy-start.19 = (s32[16]{0:T(128)S(1)}, s32[16]{0:T(128)}, u32[]{:S(2)}) copy-start(s32[16]{0:T(128)} %param.20) | copy-start | bytes 196
  3.3 20.5 %copy-start.14 = (bf16[2,3,256]{2,0,1:T(2,128)(2,1)S(1)}, bf16[2,3,256]{2,0,1:T(2,128)(2,1)}, u32[]{:S(2)}) copy-start(bf16[2,3,256]{2,0,1:T(2,128)(2,1)} %param.37) | copy-start | bytes 9220
  3.3 21.1 %copy-start.15 = (bf16[2,3,2,64]{3,2,1,0:T(2,128)(2,1)S(1)}, bf16[2,3,2,64]{3,2,1,0:T(2,128)(2,1)}, u32[]{:S(2)}) copy-start(bf16[2,3,2,64]{3,2,1,0:T(2,128)(2,1)} %param.36) | copy-start | bytes 4612
  3.3 21.9 %copy-start.17 = (s32[4,16]{1,0:T(4,128)S(1)}, s32[4,16]{1,0:T(4,128)}, u32[]{:S(2)}) copy-start(s32[4,16]{1,0:T(4,128)} %param.19) | copy-start | bytes 772
  4.5 59.5 %all-to-all-start = ((bf16[16,288,128]{2,1,0:T(8,128)(2,1)}), bf16[16,288,128]{2,1,0:T(8,128)(2,1)S(1)}, u32[]{:S(2)}, u32[]{:S(2)}) async-start(bf16[16,288,128]{2,1,0:T(8,128)(2,1)} %fusion.5), calls=%async_computation | async-start | bytes 2359296 | tf_op jit(solution)/shard_map/all_to_all | solution.py:15
  17.9 45.5 %copy-start.20 = (f32[2]{0:T(128)S(1)}, f32[2]{0:T(128)}, u32[]{:S(2)}) copy-start(f32[2]{0:T(128)} %param.30) | copy-start | bytes 28
  65.9 22.4 %all-to-all-start.1 = ((bf16[64,10,128]{2,1,0:T(8,128)(2,1)}), bf16[64,10,128]{2,1,0:T(8,128)(2,1)S(1)}, u32[]{:S(2)}, u32[]{:S(2)}) async-start(bf16[64,10,128]{2,1,0:T(8,128)(2,1)} %broadcast_in_dim.40), calls=%async_computation.1 | async-start | bytes 524288 | tf_op jit(solution)/shard_map/all_to_all | solution.py:15
  88.3 19.8 %all-to-all-start.2 = ((bf16[8,144,128]{2,1,0:T(8,128)(2,1)}), bf16[8,144,128]{2,1,0:T(8,128)(2,1)}, u32[]{:S(2)}, u32[]{:S(2)}) async-start(bf16[8,144,128]{2,1,0:T(8,128)(2,1)} %broadcast_select_fusion), calls=%async_computation.2 | async-start | bytes 589824 | tf_op jit(solution)/shard_map/all_to_all | solution.py:15
  93.8 0.5 copy-start.16
  103.3 0.6 copy-start.4
  104.0 3.6 %copy-start.8 = (f32[2,1,256]{2,0,1:T(2,128)S(1)}, f32[2,1,256]{2,0,1:T(2,128)}, u32[]{:S(2)}) copy-start(f32[2,1,256]{2,0,1:T(2,128)} %get-tuple-element.49) | copy-start | bytes 6148
  104.0 3.6 %copy-start.7 = (f32[2,1,256]{2,0,1:T(2,128)S(1)}, f32[2,1,256]{2,0,1:T(2,128)}, u32[]{:S(2)}) copy-start(f32[2,1,256]{2,0,1:T(2,128)} %get-tuple-element.48) | copy-start | bytes 6148
  104.0 3.6 %copy-start.6 = (f32[2,1,256]{2,0,1:T(2,128)S(1)}, f32[2,1,256]{2,0,1:T(2,128)}, u32[]{:S(2)}) copy-start(f32[2,1,256]{2,0,1:T(2,128)} %get-tuple-element.47) | copy-start | bytes 6148
  104.0 3.6 %copy-start.5 = (f32[2,1,256]{2,0,1:T(2,128)S(1)}, f32[2,1,256]{2,0,1:T(2,128)}, u32[]{:S(2)}) copy-start(f32[2,1,256]{2,0,1:T(2,128)} %get-tuple-element.46) | copy-start | bytes 6148
  104.1 4.9 %copy-start.12 = (f32[4,2,64]{2,1,0:T(2,128)S(1)}, f32[4,2,64]{2,1,0:T(2,128)}, u32[]{:S(2)}) copy-start(f32[4,2,64]{2,1,0:T(2,128)} %param.25) | copy-start | bytes 6148
  104.2 5.8 %copy-start.13 = (f32[4,256]{1,0:T(4,128)S(1)}, f32[4,256]{1,0:T(4,128)}, u32[]{:S(2)}) copy-start(f32[4,256]{1,0:T(4,128)} %param.27) | copy-start | bytes 12292
  104.2 5.8 %copy-start.18 = (f32[256]{0:T(256)S(1)}, f32[256]{0:T(256)}, u32[]{:S(2)}) copy-start(f32[256]{0:T(256)} %param.28) | copy-start | bytes 3076
  104.4 9.1 %copy-start.1 = (bf16[4096,128]{1,0:T(8,128)(2,1)S(1)}, bf16[4096,128]{1,0:T(8,128)(2,1)}, u32[]{:S(2)}) copy-start(bf16[4096,128]{1,0:T(8,128)(2,1)} %copy.272) | copy-start | bytes 3145732
  107.5 3.3 %copy-start.9 = (f32[2,2]{1,0:T(2,128)}, f32[2,2]{1,0:T(2,128)S(1)}, u32[]{:S(2)}) copy-start(f32[2,2]{1,0:T(2,128)S(1)} %get-tuple-element.14) | copy-start | bytes 52
  107.6 3.3 %copy-start.10 = (f32[2,2]{1,0:T(2,128)}, f32[2,2]{1,0:T(2,128)S(1)}, u32[]{:S(2)}) copy-start(f32[2,2]{1,0:T(2,128)S(1)} %get-tuple-element.40) | copy-start | bytes 52
  107.6 3.3 %copy-start.11 = (f32[2,2]{1,0:T(2,128)}, f32[2,2]{1,0:T(2,128)S(1)}, u32[]{:S(2)}) copy-start(f32[2,2]{1,0:T(2,128)S(1)} %get-tuple-element.42) | copy-start | bytes 52
  111.8 20.6 %copy-start.2 = (f32[2,2,64,128]{3,2,1,0:T(8,128)}, f32[2,2,64,128]{3,2,1,0:T(8,128)S(1)}, u32[]{:S(2)}) copy-start(f32[2,2,64,128]{3,2,1,0:T(8,128)S(1)} %multiply_add_fusion) | copy-start | bytes 393220
